TPU v7x, 256 devices: a whole 4x4x8 slice. The times are simulated.
256 devices in a mesh: row: 16 (over z, y_lo), col: 16 (over y_hi, x, core).
Axes of the slice: x: 4, y: 4 (y_hi: 2, y_lo: 2; y = y_hi * 2 + y_lo), z: 8, core: 2. Of those that a mesh axis runs over, the one named last changes fastest.
Arguments:
- separator_inverse: float32 [6144, 6144], P('row', 'col')
- panels: float32 [6144, 2048], P(('row', 'col')), as said below
- diag_inverse: float32 [2, 1024, 1024], P(None, ('row', 'col'))
- ancestors: int32 [2, 6], replicated, may hold values from 0 to 47, as said below
Outputs:
- off_blocks: float32 [6144, 2048], P(('row', 'col'))
- diag_blocks: float32 [2, 1024, 1024], P(None, ('row', 'col'))
Inputs may be any that keep to these rules, and one draw needn't show every extreme that they name: `ancestors`: each row holds 6 different tile rows of the separator in rising order. `panels`: rows of supernode s's columns are zero outside the tiles listed in ancestors[s].
All inputs are finite; a program needn't handle non-finite values.
Results may differ from a plain program's by a relative error of at most 0.00007.
Values sent between devices are 32-bit elements; how exact they have to be, the bound alone decides.
A program may use at most 64 MiB of HBM per device.

v0:
```python
import jax
import jax.numpy as jnp
from jax import lax
from jax.sharding import PartitionSpec as P

B = 128


HIGHEST = lax.Precision.HIGHEST


def broadcast(value, axis, source):
    kept = jnp.where(lax.axis_index(axis) == source, value, 0).astype(value.dtype)
    return lax.psum(kept, axis)


def per_device(separator_inverse, panels, diag_inverse, ancestors):
    rows_count = lax.axis_size("row")
    cols_count = lax.axis_size("col")
    row_id = lax.axis_index("row")
    col_id = lax.axis_index("col")
    own_rows = panels.shape[0]
    panel_width = panels.shape[1] // 2
    row_ratio = rows_count // cols_count
    row_panel = lax.all_gather(panels, "col", axis=0, tiled=True)
    pieces = broadcast(row_panel, "row", col_id * row_ratio + 0)
    reduced = lax.psum_scatter(
        jnp.dot(separator_inverse, pieces, precision=HIGHEST, preferred_element_type=jnp.float32),
        "col",
        scatter_dimension=0,
        tiled=True,
    )
    local_quad = jnp.einsum(
        "nsi,nsj->sij",
        panels.reshape(own_rows, 2, panel_width),
        reduced.reshape(own_rows, 2, panel_width),
        precision=HIGHEST,
    )
    quad_rows = lax.psum_scatter(local_quad, ("row", "col"), scatter_dimension=1, tiled=True)
    global_rows = (row_id * cols_count + col_id) * own_rows + jnp.arange(own_rows, dtype=jnp.int32)
    tile_ids = global_rows // B
    live_mask = jnp.any(tile_ids[:, None, None] == ancestors[None, :, :], axis=2).astype(
        jnp.float32
    )
    off_blocks = -(reduced.reshape(own_rows, 2, panel_width) * live_mask[:, :, None]).reshape(
        own_rows, 2 * panel_width
    )
    return (off_blocks, diag_inverse + quad_rows)


def solution(mesh):
    return jax.shard_map(
        per_device,
        mesh=mesh,
        in_specs=(P("row", "col"), P(("row", "col"), None), P(None, ("row", "col"), None), P()),
        out_specs=(P(("row", "col"), None), P(None, ("row", "col"), None)),
        check_vma=False,
    )
```

profile of v0, /device:TPU:1, one launch (start us, length us, event | category | flops | bytes accessed | tf_op | source)
XLA Modules:
  0.0 641.7 jit_solution(10026934831942300925)
XLA Ops:
  7.2 0.0 copy-start
  7.2 0.0 all-gather.2.cloned.1.call-start
  7.2 0.7 all-gather.2.cloned.1.call-update
  7.9 0.0 all-reduce.4.cloned.1.call-start
  8.0 64.4 %all-gather.2.cloned.1.call-done = f32[384,2048]{1,0:T(8,128)} async-done(((f32[24,2048]{1,0:T(8,128)}), f32[384,2048]{1,0:T(8,128)}) %all-gather.2.cloned.1.call-update) | async-done | bytes 3145744 | tf_op jit(solution)/shard_map/all_gather | solution.py:25
  72.4 2.1 broadcast_select_fusion
  74.5 0.0 all-reduce.4.cloned.1.call-update
  74.5 0.0 reduce-scatter.4.cloned.1.call-start
  74.5 157.7 %all-reduce.4.cloned.1.call-done = f32[384,2048]{1,0:T(8,128)} async-done(((f32[384,2048]{1,0:T(8,128)}), f32[384,2048]{1,0:T(8,128)}) %all-reduce.4.cloned.1.call-update) | async-done | bytes 3145744 | tf_op jit(solution)/shard_map/psum | solution.py:14
  232.2 0.0 copy-done
  232.2 12.7 %convolution_bitcast_fusion.1 = f32[384,2048]{0,1:T(8,128)} fusion(f32[384,2048]{1,0:T(8,128)} %all-reduce.4.cloned.1.call-done, f32[384,384]{1,0:T(8,128)S(1)} %copy-done), kind=kOutput, calls=%fused_computation.1 | convolution fusion | flops 3623878656 | bytes 6881280 | tf_op jit(solution)/shard_map/dot_general | solution.py:28
  244.9 3.6 copy.24
  248.5 0.0 copy-start.1
  248.5 0.0 reduce-scatter.4.cloned.1.call-update
  248.6 0.0 all-reduce.6.cloned.1.call-start
  248.6 84.2 %reduce-scatter.4.cloned.1.call-done = f32[24,2048]{1,0:T(8,128)} async-done(((f32[384,2048]{1,0:T(8,128)}), f32[24,2048]{1,0:T(8,128)}) %reduce-scatter.4.cloned.1.call-update) | async-done | bytes 196624
  332.8 1.3 copy.25
  334.1 0.0 copy-done.1
  334.1 8.8 %convolution_bitcast_fusion = f32[2,1024,1024]{1,2,0:T(8,128)} fusion(f32[24,2,1024]{0,2,1:T(8,128)S(1)} %bitcast.17, f32[3,2,8,1024]{3,2,1,0:T(8,128)S(1)} %bitcast.18), kind=kOutput, calls=%fused_computation | convolution fusion | flops 603979776 | bytes 8781824 | tf_op jit(solution)/shard_map/nsi,nsj->sij/dot_general | solution.py:33
  342.9 13.4 %copy.19 = f32[2,1024,1024]{2,0,1:T(2,128)} copy(f32[2,1024,1024]{1,2,0:T(8,128)} %convolution_bitcast_fusion) | data formatting | bytes 16777216 | tf_op jit(solution)/shard_map/nsi,nsj->sij/dot_general | solution.py:33
  356.2 0.0 copy-start.3
  356.3 0.0 all-reduce.6.cloned.1.call-update
  356.3 0.0 copy-start.2
  356.3 0.6 copy-done.3
  356.9 0.1 compare_reduce_fusion
  357.0 0.1 fusion
  357.1 1.0 copy.21
  358.1 275.6 %all-reduce.6.cloned.1.call-done = f32[2,1024,1024]{2,0,1:T(2,128)} async-done(((f32[2,1024,1024]{2,0,1:T(2,128)}), f32[2,1024,1024]{2,0,1:T(2,128)}) %all-reduce.6.cloned.1.call-update) | async-done | bytes 8388624
  633.7 0.0 copy-done.2
  633.7 0.8 dynamic-slice_add_fusion
  634.5 0.6 copy.22
  (2 shorter events, 0.0 us)
Async XLA Ops:
  7.2 225.0 %copy-start = (f32[384,384]{1,0:T(8,128)S(1)}, f32[384,384]{1,0:T(8,128)}, u32[]{:S(2)}) copy-start(f32[384,384]{1,0:T(8,128)} %param.4) | copy-start | bytes 1769476
  7.2 65.2 %all-gather.2.cloned.1.call-start = ((), (), s32[]{:S(2)}) async-start(), calls=%async_computation.1 | async-start | bytes 3342336 | tf_op jit(solution)/shard_map/all_gather | solution.py:25
  7.9 224.3 %all-reduce.4.cloned.1.call-start = ((), (), s32[]{:S(2)}) async-start(), calls=%async_computation.2 | async-start | bytes 6291456 | tf_op jit(solution)/shard_map/psum | solution.py:14
  74.5 258.4 %reduce-scatter.4.cloned.1.call-start = ((), (), s32[]{:S(2)}) async-start(), calls=%async_computation.3 | async-start | bytes 3342336
  248.5 85.6 %copy-start.1 = (f32[24,2048]{1,0:T(8,128)S(1)}, f32[24,2048]{1,0:T(8,128)}, u32[]{:S(2)}) copy-start(f32[24,2048]{1,0:T(8,128)} %param.5) | copy-start | bytes 589828
  248.6 385.2 %all-reduce.6.cloned.1.call-start = ((), (), s32[]{:S(2)}) async-start(), calls=%async_computation.4 | async-start | bytes 16777216
  356.2 0.7 copy-start.3
  356.3 277.5 %copy-start.2 = (f32[2,4,1024]{2,1,0:T(4,128)S(1)}, f32[2,4,1024]{2,1,0:T(4,128)}, u32[]{:S(2)}) copy-start(f32[2,4,1024]{2,1,0:T(4,128)} %param.6) | copy-start | bytes 98308
Sparse Core Ops, SparseCore 0:
  10.7 61.6 all-gather.1
  75.1 157.0 all-reduce.3
  248.7 84.1 reduce-scatter.3
  356.4 277.2 all-reduce.5
where the time goes:
time: 643 us; the launch traced here: 642 us
  waiting for transfers between devices  583 us (91%)
  matrix products  21.5 us (3%)
  local copies, waits for them, and re-layouts  20.4 us (3%)
  between operations  13.8 us (2%)
    unnamed x6, waiting for transfers between devices  361 us
    psum x1, waiting for transfers between devices, broadcast(): return lax.psum(kept, axis)  158 us
    all_gather x1, waiting for transfers between devices, per_device(): row_panel = lax.all_gather(panels, 'col', axis=0, tiled=True)  64.4 us
    dot_general x1, local copies, waits for them, and re-layouts, per_device(): jnp.einsum('nsi,nsj->sij', panels.reshape(own_rows, 2, panel_width), redu...  13.4 us
  transfers between devices with their start and end apart: 4, of which 4 were waited for; matrix products, arithmetic and copies ran while one was open for 0% of the time, Pallas kernels for 0%

commit v1 on v0

v1 whole, which is shorter than its diff:
```python
import jax
import jax.numpy as jnp
from jax import lax
from jax.experimental import pallas as pl
from jax.experimental.pallas import tpu as pltpu
from jax.sharding import PartitionSpec as P

MESH = pl.DeviceIdType.MESH
F32 = jnp.float32
BF16 = jnp.bfloat16
N = 16
HALF = 8
NT = 48
NA = 6
T = 128

S1, P1, X2, Y2, S2, S3, Q4, O4, D5 = range(9)


def split(x):
    high = x.astype(BF16)
    return high, (x - high.astype(F32)).astype(BF16)


def dot3(a, b):
    ah, al = a
    bh, bl = b
    dot = lambda u, v: jnp.dot(u, v, preferred_element_type=F32)
    return dot(ah, bh) + (dot(ah, bl) + dot(al, bh))


def kernel(
    anc,
    sep,
    pan,
    off,
    quad,
    s_rows,
    p_rows,
    p_unit,
    x_buf,
    y_buf,
    s_by_tile,
    s_col,
    s_tiles,
    s_unit,
    s_fin,
    q_unit,
    q_buf,
    off_st,
    d_st,
    y_hi,
    y_lo,
    send,
    recv,
):
    r = lax.axis_index("row")
    c = lax.axis_index("col")
    s = lax.div(r, HALF)
    b = lax.rem(r, HALF)

    def remote(src, dst, i, device):
        return pltpu.make_async_remote_copy(
            src_ref=src,
            dst_ref=dst,
            send_sem=send.at[i],
            recv_sem=recv.at[i],
            device_id=device,
            device_id_type=MESH,
        )

    def push(src, dst, i, dr, dc):
        here = jnp.logical_and(dr == r, dc == c)

        @pl.when(here)
        def _():
            pltpu.make_async_copy(src, dst, recv.at[i]).start()

        @pl.when(jnp.logical_not(here))
        def _():
            remote(src, dst, i, (dr, dc)).start()

    def take(sem, ref):
        pltpu.make_async_copy(ref, ref, sem).wait()

    def loop(lo, hi, body):
        def step(i, carry):
            body(i)
            return carry

        lax.fori_loop(lo, hi, step, 0)

    def send_s(i):
        d = lax.rem(c + i, N)
        remote(sep.at[:, pl.ds(8 * d, 8), :], s_rows.at[c], S1, (r, d)).start()

    loop(1, N, send_s)
    pltpu.make_async_copy(sep.at[:, pl.ds(8 * c, 8), :], s_rows.at[c], recv.at[S1]).start()

    for q in range(3):
        piece = 3 * c + q
        m = lax.div(piece, N)
        o = lax.rem(piece, N)

        def send_p(i, q=q, m=m, o=o):
            d = lax.rem(r + i, N)
            push(pan.at[q, :, pl.ds(pl.multiple_of(T * d, T), T)], p_rows.at[3 * r + m], P1, d, o)

        loop(0, N, send_p)

    take(recv.at[P1], p_rows)
    for k in range(NA):
        p_unit[k] = p_rows[anc[s, k]]

    def send_x(i):
        d = lax.rem(c + i, N)
        remote(p_unit, x_buf.at[:, c], X2, (r, d)).start()

    loop(1, N, send_x)
    x_buf[:, pl.ds(c, 1)] = p_unit[...][:, None]

    def send_y(i):
        dr = HALF * s + lax.rem(b + lax.div(i, 2), HALF)
        push(p_unit, y_buf.at[:, c], Y2, dr, 2 * b + lax.rem(i, 2))

    loop(0, 2 * HALF, send_y)

    take(recv.at[S1], s_rows)
    for j in range(N):
        for v in range(3):
            s_by_tile[3 * j + v] = s_rows[j, :, :, T * v : T * v + T]
    for t in range(2):
        for l in range(NA):
            s_col[t, l] = s_by_tile[anc[t, l]]

    def send_s2(i):
        t = lax.div(i, NA)
        l = lax.rem(i, NA)
        push(s_col.at[t, l], s_tiles.at[pl.ds(3 * r, 3)], S2, HALF * t + l, c)

    loop(0, 2 * NA, send_s2)

    @pl.when(b < NA)
    def _():
        take(recv.at[S2], s_tiles)
        for k in range(NA):
            s_unit[k] = s_tiles[anc[s, k]]

        def send_s3(i):
            d = HALF * s + lax.rem(b + i, HALF)
            remote(s_unit, s_fin.at[b], S3, (d, c)).start()

        loop(1, HALF, send_s3)
        pltpu.make_async_copy(s_unit, s_fin.at[b], recv.at[S3]).start()

    take(recv.at[Y2], y_buf)
    for k in range(NA):
        yt = y_buf[k].reshape(T, T).T
        hi, lo = split(yt)
        y_hi[k] = hi
        y_lo[k] = lo

    take(recv.at[X2], x_buf.at[:, pl.ds(0, N - 1)])
    take(recv.at[S3], s_fin)
    acc = jnp.zeros((NA * 8, T), F32)
    for l in range(NA):
        acc += dot3(split(s_fin[l].reshape(NA * 8, T)), split(x_buf[l].reshape(T, T)))
    q_unit[pl.ds(0, NA)] = acc.reshape(NA, 8, T)
    q_unit[NA] = jnp.zeros((8, T), F32)

    def send_q(i):
        d = lax.rem(c + i, N)
        remote(q_unit.at[pl.ds(0, NA)], q_buf.at[:, c], Q4, (r, d)).start()

    loop(1, N, send_q)
    q_buf[:, pl.ds(c, 1)] = q_unit[pl.ds(0, NA)][:, None]

    for t in range(NT):
        place = NA
        for k in range(NA):
            place = jnp.minimum(place, NA - (anc[s, k] == t).astype(jnp.int32) * (NA - k))
        off_st[t] = -q_unit[place]

    def send_off(i):
        t = lax.rem(3 * r + i, NT)
        piece = N * lax.rem(t, 3) + c
        dst = off.at[lax.rem(piece, 3), :, pl.ds(pl.multiple_of(T * r, T), T)]
        push(off_st.at[t], dst, O4, lax.div(t, 3), lax.div(piece, 3))

    loop(0, NT, send_off)

    take(recv.at[Q4], q_buf.at[:, pl.ds(0, N - 1)])
    rows = pl.ds(pl.multiple_of(lax.rem(c, 2) * 64, 64), 64)
    acc = jnp.zeros((64, T), F32)
    for k in range(NA):
        acc += dot3((y_hi[k, rows, :], y_lo[k, rows, :]), split(q_buf[k].reshape(T, T)))
    d_st[...] = acc.reshape(N, 4, T)

    def send_d(i):
        d = lax.rem(c + i, N)
        push(d_st.at[d], quad.at[r], D5, c, d)

    loop(0, N, send_d)

    take(send.at[S1], s_rows.at[pl.ds(0, N - 1)])
    take(send.at[X2], x_buf.at[:, pl.ds(0, N - 1)])
    take(send.at[Q4], q_buf.at[:, pl.ds(0, N - 1)])

    @pl.when(b < NA)
    def _():
        take(send.at[S3], s_tiles.at[pl.ds(0, 7 * NA)])
        take(send.at[S2], s_tiles.at[pl.ds(0, 33)])

    @pl.when(b >= NA)
    def _():
        take(send.at[S2], s_tiles.at[pl.ds(0, 36)])

    own = jnp.logical_or(jnp.logical_or(c == 0, c == 7), jnp.logical_or(c == 8, c == 15))

    @pl.when(own)
    def _():
        take(send.at[P1], p_rows.at[pl.ds(0, NT - 1)])
        take(send.at[O4], p_rows.at[pl.ds(0, NT - 1)])

    @pl.when(jnp.logical_not(own))
    def _():
        take(send.at[P1], p_rows)
        take(send.at[O4], p_rows)

    @pl.when(lax.div(c, 2) == b)
    def _():
        take(send.at[Y2], y_buf.at[:, pl.ds(0, N - 1)])

    @pl.when(lax.div(c, 2) != b)
    def _():
        take(send.at[Y2], y_buf)

    @pl.when(r == c)
    def _():
        take(send.at[D5], d_st.at[pl.ds(0, N - 1)])

    @pl.when(r != c)
    def _():
        take(send.at[D5], d_st)

    take(recv.at[O4], off)
    take(recv.at[D5], quad)


def per_device(separator_inverse, panels, diag_inverse, ancestors):
    hbm = pl.BlockSpec(memory_space=pl.ANY)
    vmem = pltpu.VMEM
    off, quad = pl.pallas_call(
        kernel,
        out_shape=(
            jax.ShapeDtypeStruct((3, 8, 2 * HALF * T), F32),
            jax.ShapeDtypeStruct((N, 4, T), F32),
        ),
        in_specs=[pl.BlockSpec(memory_space=pltpu.SMEM), hbm, hbm],
        out_specs=(hbm, pl.BlockSpec(memory_space=pltpu.VMEM)),
        scratch_shapes=[
            vmem((N, 3, 8, 3 * T), F32),
            vmem((NT, 8, T), F32),
            vmem((NA, 8, T), F32),
            vmem((NA, N, 8, T), F32),
            vmem((NA, N, 8, T), F32),
            vmem((NT, 3, 8, T), F32),
            vmem((2, NA, 3, 8, T), F32),
            vmem((NT, 8, T), F32),
            vmem((NA, 8, T), F32),
            vmem((NA, NA, 8, T), F32),
            vmem((NA + 1, 8, T), F32),
            vmem((NA, N, 8, T), F32),
            vmem((NT, 8, T), F32),
            vmem((N, 4, T), F32),
            vmem((NA, T, T), BF16),
            vmem((NA, T, T), BF16),
            pltpu.SemaphoreType.DMA((9,)),
            pltpu.SemaphoreType.DMA((9,)),
        ],
        compiler_params=pltpu.CompilerParams(has_side_effects=True),
        name="selected_inverse",
    )(
        ancestors,
        separator_inverse.reshape(3, T, 3 * T),
        panels.reshape(3, 8, 2 * HALF * T),
    )
    quad_rows = quad.reshape(2, HALF, 4, T).transpose(0, 2, 1, 3).reshape(2, 4, HALF * T)
    return off.reshape(24, 2 * HALF * T), diag_inverse + quad_rows


def solution(mesh):
    return jax.shard_map(
        per_device,
        mesh=mesh,
        in_specs=(P("row", "col"), P(("row", "col"), None), P(None, ("row", "col"), None), P()),
        out_specs=(P(("row", "col"), None), P(None, ("row", "col"), None)),
        check_vma=False,
    )
```

time: 643 us -> 72.9 us (0.11)
  waiting for transfers between devices: 583 us -> 0 us
  Pallas kernels: 0 us -> 67.9 us
  matrix products: 21.5 us -> 0 us
  local copies, waits for them, and re-layouts: 20.4 us -> 1.62 us
  between operations: 13.8 us -> 0.66 us
    unnamed x6 -> x0, waiting for transfers between devices: 361 us -> none
    psum x1 -> x0, waiting for transfers between devices: 158 us -> none  [broadcast(): return lax.psum(kept, axis)]
    pallas_call x0 -> x1, Pallas kernels: none -> 67.9 us  [per_device(): pl.pallas_call(kernel, out_shape=(jax.ShapeDtypeStruct((3, 8, 2 * HALF *...]
    all_gather x1 -> x0, waiting for transfers between devices: 64.4 us -> none  [per_device(): row_panel = lax.all_gather(panels, 'col', axis=0, tiled=True)]
    dot_general x2 -> x0, matrix products: 21.5 us -> none  [the longest x1 12.7 us: per_device(): jnp.dot(separator_inverse, pieces, precision=HIGHEST, preferred_element_t...]
    dot_general x1 -> x0, local copies, waits for them, and re-layouts: 13.4 us -> none  [per_device(): jnp.einsum('nsi,nsj->sij', panels.reshape(own_rows, 2, panel_width), redu...]
  transfers between devices with their start and end apart: 4 -> 0, of which waited for: 4 -> 0; matrix products, arithmetic and copies ran while one was open for 0% -> 0% of each run, Pallas kernels for 0% -> 0%
where the time goes in v1:
time: 72.9 us; the launch traced here: 71.5 us
  Pallas kernels  67.9 us (93%)
  local copies, waits for them, and re-layouts  1.62 us (2%)
  other arithmetic  1.38 us (2%)
    pallas_call x1, Pallas kernels, per_device(): pl.pallas_call(kernel, out_shape=(jax.ShapeDtypeStruct((3, 8, 2 * HALF *...  67.9 us
    unnamed x3, local copies, waits for them, and re-layouts  1.62 us

profile of v1, /device:TPU:1, one launch (start us, length us, event | category | flops | bytes accessed | tf_op | source)
XLA Modules:
  0.0 71.5 jit_solution(7233701487518806649)
XLA Ops:
  0.6 0.0 copy-start
  0.6 67.9 %selected_inverse.1 = (f32[3,8,2048]{2,1,0:T(8,128)}, f32[16,4,128]{2,1,0:T(4,128)}) custom-call(s32[2,6]{1,0:T(2,128)} %anc.1, f32[3,128,384]{2,1,0:T(8,128)} %bitcast.8, f32[3,8,2048]{2,1,0:T(8,128)} %bitcast.10), custom_call_target="tpu_custom_call" | custom-call | tf_op jit(solution)/shard_map/selected_inverse/pallas_call | solution.py:253
  68.5 0.0 copy-done
  68.5 1.4 %add.3 = f32[2,4,1024]{2,1,0:T(4,128)} add(f32[2,4,1024]{2,1,0:T(4,128)S(1)} %copy-done, f32[2,4,1024]{2,1,0:T(4,128)} %bitcast.11) | non-fusion elementwise | flops 8192 | bytes 98304 | tf_op jit(solution)/shard_map/add | solution.py:289
  69.9 1.6 %copy.8 = f32[24,2048]{1,0:T(8,128)} copy(f32[24,2048]{1,0:T(8,128)} %bitcast.9) | data formatting | bytes 393216
Async XLA Ops:
  0.6 67.9 %copy-start = (f32[2,4,1024]{2,1,0:T(4,128)S(1)}, f32[2,4,1024]{2,1,0:T(4,128)}, u32[]{:S(2)}) copy-start(f32[2,4,1024]{2,1,0:T(4,128)} %param.6) | copy-start | bytes 98308

commit v2 on v1

--- a/solution.py
+++ b/solution.py
@@ -14,7 +14,7 @@
 NA = 6
 T = 128
 
-S1, P1, X2, Y2, S2, S3, Q4, O4, D5 = range(9)
+BAR, S1, S2, S3, P1, P2, X3, Y3, Y4, Q4, O4, O5, D5 = range(13)
 
 
 def split(x):
@@ -36,21 +36,25 @@
     off,
     quad,
     s_rows,
-    p_rows,
-    p_unit,
-    x_buf,
-    y_buf,
     s_by_tile,
     s_col,
     s_tiles,
     s_unit,
     s_fin,
+    p_cols,
+    p_perm,
+    p_rows,
+    p_unit,
+    x_buf,
+    y_units,
+    y_buf,
+    y_hi,
+    y_lo,
     q_unit,
     q_buf,
     off_st,
+    off_cols,
     d_st,
-    y_hi,
-    y_lo,
     send,
     recv,
 ):
@@ -69,12 +73,15 @@
             device_id_type=MESH,
         )
 
+    def local(src, dst, i):
+        return pltpu.make_async_copy(src, dst, recv.at[i])
+
     def push(src, dst, i, dr, dc):
         here = jnp.logical_and(dr == r, dc == c)
 
         @pl.when(here)
         def _():
-            pltpu.make_async_copy(src, dst, recv.at[i]).start()
+            local(src, dst, i).start()
 
         @pl.when(jnp.logical_not(here))
         def _():
@@ -90,40 +97,39 @@
 
         lax.fori_loop(lo, hi, step, 0)
 
+    barrier = pltpu.get_barrier_semaphore()
+
+    def greet(i):
+        for device in ((lax.rem(r + i, N), c), (r, lax.rem(c + i, N))):
+            pl.semaphore_signal(barrier, inc=1, device_id=device, device_id_type=MESH)
+
+    loop(1, N, greet)
+    pl.semaphore_wait(barrier, 2 * (N - 1))
+
     def send_s(i):
         d = lax.rem(c + i, N)
         remote(sep.at[:, pl.ds(8 * d, 8), :], s_rows.at[c], S1, (r, d)).start()
 
     loop(1, N, send_s)
-    pltpu.make_async_copy(sep.at[:, pl.ds(8 * c, 8), :], s_rows.at[c], recv.at[S1]).start()
-
-    for q in range(3):
+    local(sep.at[:, pl.ds(8 * c, 8), :], s_rows.at[c], S1).start()
+
+    def columns(d):
+        return pan.at[:, :, pl.ds(pl.multiple_of(T * d, T), T)]
+
+    def send_p(i):
+        d = lax.rem(r + i, N)
+        remote(columns(d), p_cols.at[r], P1, (d, c)).start()
+
+    loop(1, N, send_p)
+    local(columns(r), p_cols.at[r], P1).start()
+
+    take(recv.at[P1], p_cols)
+
+    def send_p2(q):
         piece = 3 * c + q
-        m = lax.div(piece, N)
-        o = lax.rem(piece, N)
-
-        def send_p(i, q=q, m=m, o=o):
-            d = lax.rem(r + i, N)
-            push(pan.at[q, :, pl.ds(pl.multiple_of(T * d, T), T)], p_rows.at[3 * r + m], P1, d, o)
-
-        loop(0, N, send_p)
-
-    take(recv.at[P1], p_rows)
-    for k in range(NA):
-        p_unit[k] = p_rows[anc[s, k]]
-
-    def send_x(i):
-        d = lax.rem(c + i, N)
-        remote(p_unit, x_buf.at[:, c], X2, (r, d)).start()
-
-    loop(1, N, send_x)
-    x_buf[:, pl.ds(c, 1)] = p_unit[...][:, None]
-
-    def send_y(i):
-        dr = HALF * s + lax.rem(b + lax.div(i, 2), HALF)
-        push(p_unit, y_buf.at[:, c], Y2, dr, 2 * b + lax.rem(i, 2))
-
-    loop(0, 2 * HALF, send_y)
+        push(p_cols.at[:, q], p_perm.at[lax.div(piece, N)], P2, r, lax.rem(piece, N))
+
+    loop(0, 3, send_p2)
 
     take(recv.at[S1], s_rows)
     for j in range(N):
@@ -140,6 +146,27 @@
 
     loop(0, 2 * NA, send_s2)
 
+    take(recv.at[P2], p_perm)
+    for j in range(N):
+        for m in range(3):
+            p_rows[3 * j + m] = p_perm[m, j]
+    for k in range(NA):
+        p_unit[k] = p_rows[anc[s, k]]
+
+    def send_x(i):
+        d = lax.rem(c + i, N)
+        remote(p_unit, x_buf.at[:, c], X3, (r, d)).start()
+
+    loop(1, N, send_x)
+    x_buf[:, pl.ds(c, 1)] = p_unit[...][:, None]
+
+    def send_y(i):
+        d = HALF * s + lax.rem(b + i, HALF)
+        remote(p_unit, y_units.at[b], Y3, (d, c)).start()
+
+    loop(1, HALF, send_y)
+    local(p_unit, y_units.at[b], Y3).start()
+
     @pl.when(b < NA)
     def _():
         take(recv.at[S2], s_tiles)
@@ -151,16 +178,18 @@
             remote(s_unit, s_fin.at[b], S3, (d, c)).start()
 
         loop(1, HALF, send_s3)
-        pltpu.make_async_copy(s_unit, s_fin.at[b], recv.at[S3]).start()
-
-    take(recv.at[Y2], y_buf)
-    for k in range(NA):
-        yt = y_buf[k].reshape(T, T).T
-        hi, lo = split(yt)
-        y_hi[k] = hi
-        y_lo[k] = lo
-
-    take(recv.at[X2], x_buf.at[:, pl.ds(0, N - 1)])
+        local(s_unit, s_fin.at[b], S3).start()
+
+    take(recv.at[Y3], y_units)
+
+    def send_y4(i):
+        d = lax.rem(c + i, N)
+        remote(y_units.at[lax.div(d, 2)], y_buf.at[:, c], Y4, (r, d)).start()
+
+    loop(1, N, send_y4)
+    local(y_units.at[lax.div(c, 2)], y_buf.at[:, c], Y4).start()
+
+    take(recv.at[X3], x_buf.at[:, pl.ds(0, N - 1)])
     take(recv.at[S3], s_fin)
     acc = jnp.zeros((NA * 8, T), F32)
     for l in range(NA):
@@ -182,12 +211,17 @@
         off_st[t] = -q_unit[place]
 
     def send_off(i):
-        t = lax.rem(3 * r + i, NT)
-        piece = N * lax.rem(t, 3) + c
-        dst = off.at[lax.rem(piece, 3), :, pl.ds(pl.multiple_of(T * r, T), T)]
-        push(off_st.at[t], dst, O4, lax.div(t, 3), lax.div(piece, 3))
-
-    loop(0, NT, send_off)
+        d = lax.rem(r + i, N)
+        remote(off_st.at[pl.ds(3 * d, 3)], off_cols.at[r], O4, (d, c)).start()
+
+    loop(1, N, send_off)
+    local(off_st.at[pl.ds(3 * r, 3)], off_cols.at[r], O4).start()
+
+    take(recv.at[Y4], y_buf)
+    for k in range(NA):
+        hi, lo = split(y_buf[k].reshape(T, T).T)
+        y_hi[k] = hi
+        y_lo[k] = lo
 
     take(recv.at[Q4], q_buf.at[:, pl.ds(0, N - 1)])
     rows = pl.ds(pl.multiple_of(lax.rem(c, 2) * 64, 64), 64)
@@ -202,9 +236,21 @@
 
     loop(0, N, send_d)
 
+    take(recv.at[O4], off_cols)
+
+    def send_off2(m):
+        piece = N * m + c
+        push(off_cols.at[:, m], off.at[lax.rem(piece, 3)], O5, r, lax.div(piece, 3))
+
+    loop(0, 3, send_off2)
+
     take(send.at[S1], s_rows.at[pl.ds(0, N - 1)])
-    take(send.at[X2], x_buf.at[:, pl.ds(0, N - 1)])
+    take(send.at[P1], p_cols.at[pl.ds(0, N - 1)])
+    take(send.at[X3], x_buf.at[:, pl.ds(0, N - 1)])
+    take(send.at[Y3], y_units.at[pl.ds(0, HALF - 1)])
+    take(send.at[Y4], y_buf.at[:, pl.ds(0, N - 1)])
     take(send.at[Q4], q_buf.at[:, pl.ds(0, N - 1)])
+    take(send.at[O4], off_cols.at[pl.ds(0, N - 1)])
 
     @pl.when(b < NA)
     def _():
@@ -219,21 +265,13 @@
 
     @pl.when(own)
     def _():
-        take(send.at[P1], p_rows.at[pl.ds(0, NT - 1)])
-        take(send.at[O4], p_rows.at[pl.ds(0, NT - 1)])
+        take(send.at[P2], p_perm.at[pl.ds(0, 2)])
+        take(send.at[O5], p_perm.at[pl.ds(0, 2)])
 
     @pl.when(jnp.logical_not(own))
     def _():
-        take(send.at[P1], p_rows)
-        take(send.at[O4], p_rows)
-
-    @pl.when(lax.div(c, 2) == b)
-    def _():
-        take(send.at[Y2], y_buf.at[:, pl.ds(0, N - 1)])
-
-    @pl.when(lax.div(c, 2) != b)
-    def _():
-        take(send.at[Y2], y_buf)
+        take(send.at[P2], p_perm)
+        take(send.at[O5], p_perm)
 
     @pl.when(r == c)
     def _():
@@ -243,7 +281,7 @@
     def _():
         take(send.at[D5], d_st)
 
-    take(recv.at[O4], off)
+    take(recv.at[O5], off)
     take(recv.at[D5], quad)
 
 
@@ -253,32 +291,36 @@
     off, quad = pl.pallas_call(
         kernel,
         out_shape=(
-            jax.ShapeDtypeStruct((3, 8, 2 * HALF * T), F32),
+            jax.ShapeDtypeStruct((3, N, 8, T), F32),
             jax.ShapeDtypeStruct((N, 4, T), F32),
         ),
         in_specs=[pl.BlockSpec(memory_space=pltpu.SMEM), hbm, hbm],
         out_specs=(hbm, pl.BlockSpec(memory_space=pltpu.VMEM)),
         scratch_shapes=[
             vmem((N, 3, 8, 3 * T), F32),
-            vmem((NT, 8, T), F32),
-            vmem((NA, 8, T), F32),
-            vmem((NA, N, 8, T), F32),
-            vmem((NA, N, 8, T), F32),
             vmem((NT, 3, 8, T), F32),
             vmem((2, NA, 3, 8, T), F32),
             vmem((NT, 8, T), F32),
             vmem((NA, 8, T), F32),
             vmem((NA, NA, 8, T), F32),
+            vmem((N, 3, 8, T), F32),
+            vmem((3, N, 8, T), F32),
+            vmem((NT, 8, T), F32),
+            vmem((NA, 8, T), F32),
+            vmem((NA, N, 8, T), F32),
+            vmem((HALF, NA, 8, T), F32),
+            vmem((NA, N, 8, T), F32),
+            vmem((NA, T, T), BF16),
+            vmem((NA, T, T), BF16),
             vmem((NA + 1, 8, T), F32),
             vmem((NA, N, 8, T), F32),
             vmem((NT, 8, T), F32),
+            vmem((N, 3, 8, T), F32),
             vmem((N, 4, T), F32),
-            vmem((NA, T, T), BF16),
-            vmem((NA, T, T), BF16),
-            pltpu.SemaphoreType.DMA((9,)),
-            pltpu.SemaphoreType.DMA((9,)),
+            pltpu.SemaphoreType.DMA((13,)),
+            pltpu.SemaphoreType.DMA((13,)),
         ],
-        compiler_params=pltpu.CompilerParams(has_side_effects=True),
+        compiler_params=pltpu.CompilerParams(collective_id=0, has_side_effects=True),
         name="selected_inverse",
     )(
         ancestors,
@@ -286,7 +328,8 @@
         panels.reshape(3, 8, 2 * HALF * T),
     )
     quad_rows = quad.reshape(2, HALF, 4, T).transpose(0, 2, 1, 3).reshape(2, 4, HALF * T)
-    return off.reshape(24, 2 * HALF * T), diag_inverse + quad_rows
+    off_rows = off.transpose(0, 2, 1, 3).reshape(24, 2 * HALF * T)
+    return off_rows, diag_inverse + quad_rows
 
 
 def solution(mesh):

time: 72.9 us -> 59.9 us (0.82); the launches traced: 71.5 us -> 59.3 us
  Pallas kernels: 67.9 us -> 55.6 us
    pallas_call x1, Pallas kernels: 67.9 us -> 55.6 us  [per_device(): pl.pallas_call(kernel, out_shape=(jax.ShapeDtypeStruct((3, N, 8, T), F32)...]
where the time goes in v2:
time: 59.9 us; the launch traced here: 59.3 us
  Pallas kernels  55.6 us (93%)
  local copies, waits for them, and re-layouts  1.62 us (3%)
  other arithmetic  1.38 us (2%)
  between operations  0.66 us (1%)
    pallas_call x1, Pallas kernels, per_device(): pl.pallas_call(kernel, out_shape=(jax.ShapeDtypeStruct((3, N, 8, T), F32)...  55.6 us
    unnamed x3, local copies, waits for them, and re-layouts  1.62 us
    add x1, other arithmetic, per_device(): return (off_rows, diag_inverse + quad_rows)  1.38 us

profile of v2, /device:TPU:1, one launch (start us, length us, event | category | flops | bytes accessed | tf_op | source)
XLA Modules:
  0.0 59.3 jit_solution(10133529464998654829)
XLA Ops:
  0.6 0.0 copy-start
  0.6 55.6 %selected_inverse.1 = (f32[3,16,8,128]{3,2,1,0:T(8,128)}, f32[16,4,128]{2,1,0:T(4,128)}) custom-call(s32[2,6]{1,0:T(2,128)} %anc.1, f32[3,128,384]{2,1,0:T(8,128)} %bitcast.10, f32[3,8,2048]{2,1,0:T(8,128)} %bitcast.12), custom_call_target="tpu_custom_call" | custom-call | tf_op jit(solution)/shard_map/selected_inverse/pallas_call | solution.py:291
  56.3 0.0 copy-done
  56.3 1.4 %add.3 = f32[2,4,1024]{2,1,0:T(4,128)} add(f32[2,4,1024]{2,1,0:T(4,128)S(1)} %copy-done, f32[2,4,1024]{2,1,0:T(4,128)} %bitcast.13) | non-fusion elementwise | flops 8192 | bytes 98304 | tf_op jit(solution)/shard_map/add | solution.py:332
  57.7 1.6 %copy.8 = f32[24,2048]{1,0:T(8,128)} copy(f32[24,2048]{1,0:T(8,128)} %bitcast.11) | data formatting | bytes 393216
Async XLA Ops:
  0.6 55.6 %copy-start = (f32[2,4,1024]{2,1,0:T(4,128)S(1)}, f32[2,4,1024]{2,1,0:T(4,128)}, u32[]{:S(2)}) copy-start(f32[2,4,1024]{2,1,0:T(4,128)} %param.6) | copy-start | bytes 98308

commit v3 on v2

v3 whole, which is shorter than its diff:
```python
import jax
import jax.numpy as jnp
from jax import lax
from jax.experimental import pallas as pl
from jax.experimental.pallas import tpu as pltpu
from jax.sharding import PartitionSpec as P

MESH = pl.DeviceIdType.MESH
F32 = jnp.float32
BF16 = jnp.bfloat16
N = 16
HALF = 8
NT = 48
NA = 6
T = 128

S1, S2, S3, P1, P2, X3, Y4, Q4, O5, D5 = range(10)


def split(x):
    high = x.astype(BF16)
    return high, (x - high.astype(F32)).astype(BF16)


def dot3(a, b):
    ah, al = a
    bh, bl = b
    dot = lambda u, v: jnp.dot(u, v, preferred_element_type=F32)
    return dot(ah, bh) + (dot(ah, bl) + dot(al, bh))


def kernel(
    anc,
    sep,
    pan,
    off,
    quad,
    place,
    s_rows,
    s_by_tile,
    s_col,
    s_tiles,
    s_unit,
    s_fin,
    p_cols,
    p_send,
    p_perm,
    p_unit,
    x_buf,
    x_t,
    y_unit,
    y_buf,
    q_unit,
    q_buf,
    off_st,
    d_st,
    send,
    recv,
):
    r = lax.axis_index("row")
    c = lax.axis_index("col")
    s = lax.div(r, HALF)
    b = lax.rem(r, HALF)

    def remote(src, dst, i, device):
        return pltpu.make_async_remote_copy(
            src_ref=src,
            dst_ref=dst,
            send_sem=send.at[i],
            recv_sem=recv.at[i],
            device_id=device,
            device_id_type=MESH,
        )

    def local(src, dst, i):
        return pltpu.make_async_copy(src, dst, recv.at[i])

    def push(src, dst, i, dr, dc):
        here = jnp.logical_and(dr == r, dc == c)

        @pl.when(here)
        def _():
            local(src, dst, i).start()

        @pl.when(jnp.logical_not(here))
        def _():
            remote(src, dst, i, (dr, dc)).start()

    def take(sem, ref):
        pltpu.make_async_copy(ref, ref, sem).wait()

    def loop(lo, hi, body):
        def step(i, carry):
            body(i)
            return carry

        lax.fori_loop(lo, hi, step, 0)

    def over_col(i):
        j = N - 1 - i
        half, along, core = lax.div(j, 8), lax.rem(lax.div(j, 2), 4), lax.rem(j, 2)
        along = lax.div(along * (along + 1), 2)
        return (
            8 * lax.rem(lax.div(c, 8) + half, 2)
            + 2 * lax.rem(lax.div(c, 2) + along, 4)
            + lax.rem(c + core, 2)
        )

    def over_row(i):
        j = lax.div(i, 2)
        z = 4 + (1 - 2 * lax.rem(j, 2)) * lax.div(j + 1, 2)
        return 2 * lax.rem(lax.div(r, 2) + z, HALF) + lax.rem(r + 1 + i, 2)

    def over_half(i):
        j = 3 - lax.div(i, 2)
        z = lax.div(j * (j + 1), 2)
        return HALF * s + 2 * lax.rem(lax.div(b, 2) + z, 4) + lax.rem(b + 1 + i, 2)

    barrier = pltpu.get_barrier_semaphore()

    def greet(i):
        for device in ((over_row(i), c), (r, over_col(i))):
            pl.semaphore_signal(barrier, inc=1, device_id=device, device_id_type=MESH)

    loop(0, N - 1, greet)
    pl.semaphore_wait(barrier, 2 * (N - 1))

    def send_s(i):
        d = over_col(i)
        remote(sep.at[:, pl.ds(8 * d, 8), :], s_rows.at[c], S1, (r, d)).start()

    loop(0, N - 1, send_s)
    local(sep.at[:, pl.ds(8 * c, 8), :], s_rows.at[c], S1).start()

    def columns(d):
        return pan.at[:, :, pl.ds(pl.multiple_of(T * d, T), T)]

    def send_p(i):
        d = over_row(i)
        remote(columns(d), p_cols.at[r], P1, (d, c)).start()

    loop(0, N - 1, send_p)
    local(columns(r), p_cols.at[r], P1).start()

    row_of = []
    for k in range(NA):
        value = 0
        for j in range(1, N):
            value += (anc[s, k] >= 3 * j).astype(jnp.int32)
        row_of.append(value)
    for t in range(NT):
        value = NA
        for k in range(NA):
            value = jnp.minimum(value, NA - (anc[s, k] == t).astype(jnp.int32) * (NA - k))
        place[t] = value

    take(recv.at[P1], p_cols)
    for k in range(NA):
        for q in range(3):
            p_send[q, k] = p_cols[row_of[k], q]

    def send_p2(q):
        piece = 3 * c + q
        push(p_send.at[q], p_perm.at[lax.div(piece, N)], P2, r, lax.rem(piece, N))

    loop(0, 3, send_p2)

    take(recv.at[S1], s_rows)
    for j in range(N):
        for v in range(3):
            s_by_tile[3 * j + v] = s_rows[j, :, :, T * v : T * v + T]
    for t in range(2):
        for l in range(NA):
            s_col[t, l] = s_by_tile[anc[t, l]]

    def send_s2(i):
        d = over_row(i)
        l = lax.rem(d, HALF)

        @pl.when(l < NA)
        def _():
            src = s_col.at[lax.div(d, HALF), l]
            remote(src, s_tiles.at[pl.ds(3 * r, 3)], S2, (d, c)).start()

    loop(0, N - 1, send_s2)

    @pl.when(b < NA)
    def _():
        local(s_col.at[s, b], s_tiles.at[pl.ds(3 * r, 3)], S2).start()

    take(recv.at[P2], p_perm)
    for k in range(NA):
        p_unit[k] = p_perm[anc[s, k] - 3 * row_of[k], k]

    def send_x(i):
        d = over_col(i)
        remote(p_unit, x_buf.at[:, c], X3, (r, d)).start()

    loop(0, N - 1, send_x)
    x_buf[:, pl.ds(c, 1)] = p_unit[...][:, None]

    @pl.when(b < NA)
    def _():
        take(recv.at[S2], s_tiles)
        for k in range(NA):
            s_unit[k] = s_tiles[anc[s, k]]

        def send_s3(i):
            d = over_half(i)
            remote(s_unit, s_fin.at[b], S3, (d, c)).start()

        loop(0, HALF - 1, send_s3)
        local(s_unit, s_fin.at[b], S3).start()

    take(recv.at[X3], x_buf.at[:, pl.ds(0, N - 1)])
    for k in range(NA):
        x_t[:, :, T * k : T * (k + 1)] = x_buf[k].reshape(T, T).T.reshape(2 * N, 4, T)
    y_unit[0:4] = x_t[c]
    y_unit[4:8] = x_t[N + c]

    def send_y4(i):
        d = over_half(i)
        remote(y_unit, y_buf.at[b], Y4, (d, c)).start()

    loop(0, HALF - 1, send_y4)
    local(y_unit, y_buf.at[b], Y4).start()

    take(recv.at[S3], s_fin)
    acc = jnp.zeros((NA * 8, T), F32)
    for l in range(NA):
        acc += dot3(split(s_fin[l].reshape(NA * 8, T)), split(x_buf[l].reshape(T, T)))
    q_unit[...] = acc.reshape(NA, 8, T)

    def send_q(i):
        d = over_col(i)
        remote(q_unit, q_buf.at[pl.ds(0, NA), c], Q4, (r, d)).start()

    loop(0, N - 1, send_q)
    q_buf[0:NA, pl.ds(c, 1)] = q_unit[...][:, None]
    q_buf[NA] = jnp.zeros((N, 8, T), F32)

    take(recv.at[Y4], y_buf)
    y_halves = split(y_buf[...].reshape(HALF * 8, NA * T))
    take(recv.at[Q4], q_buf.at[pl.ds(0, NA), pl.ds(0, N - 1)])

    for q in range(3):
        piece = 3 * c + q
        m, o = lax.div(piece, N), lax.rem(piece, N)
        for j in range(N):
            off_st[j, q] = -q_buf[place[3 * j + m], o]

    def send_off(i):
        d = over_row(i)
        remote(off_st.at[d], off.at[:, r], O5, (d, c)).start()

    loop(0, N - 1, send_off)
    local(off_st.at[r], off.at[:, r], O5).start()

    acc = dot3(y_halves, split(q_buf[0:NA].reshape(NA * T, T)))
    d_st[...] = acc.reshape(N, 4, T)

    def send_d(i):
        d = over_row(i)
        remote(d_st.at[d], quad.at[r], D5, (d, c)).start()

    loop(0, N - 1, send_d)
    local(d_st.at[r], quad.at[r], D5).start()

    take(send.at[S1], s_rows.at[pl.ds(0, N - 1)])
    take(send.at[P1], p_cols.at[pl.ds(0, N - 1)])
    take(send.at[X3], x_buf.at[:, pl.ds(0, N - 1)])
    take(send.at[Y4], y_buf.at[pl.ds(0, HALF - 1)])
    take(send.at[Q4], x_buf.at[:, pl.ds(0, N - 1)])
    take(send.at[O5], off_st.at[pl.ds(0, N - 1)])
    take(send.at[D5], d_st.at[pl.ds(0, N - 1)])

    @pl.when(b < NA)
    def _():
        take(send.at[S3], s_tiles.at[pl.ds(0, 7 * NA)])
        take(send.at[S2], s_tiles.at[pl.ds(0, 33)])

    @pl.when(b >= NA)
    def _():
        take(send.at[S2], s_tiles.at[pl.ds(0, 36)])

    own = jnp.logical_or(jnp.logical_or(c == 0, c == 7), jnp.logical_or(c == 8, c == 15))

    @pl.when(own)
    def _():
        take(send.at[P2], p_perm.at[pl.ds(0, 2)])

    @pl.when(jnp.logical_not(own))
    def _():
        take(send.at[P2], p_perm)

    take(recv.at[O5], off)
    take(recv.at[D5], quad)


def per_device(separator_inverse, panels, diag_inverse, ancestors):
    hbm = pl.BlockSpec(memory_space=pl.ANY)
    vmem = pltpu.VMEM
    off, quad = pl.pallas_call(
        kernel,
        out_shape=(
            jax.ShapeDtypeStruct((3, N, 8, T), F32),
            jax.ShapeDtypeStruct((N, 4, T), F32),
        ),
        in_specs=[pl.BlockSpec(memory_space=pltpu.SMEM), hbm, hbm],
        out_specs=(hbm, pl.BlockSpec(memory_space=pltpu.VMEM)),
        scratch_shapes=[
            pltpu.SMEM((NT,), jnp.int32),
            vmem((N, 3, 8, 3 * T), F32),
            vmem((NT, 3, 8, T), F32),
            vmem((2, NA, 3, 8, T), F32),
            vmem((NT, 8, T), F32),
            vmem((NA, 8, T), F32),
            vmem((NA, NA, 8, T), F32),
            vmem((N, 3, 8, T), F32),
            vmem((3, NA, 8, T), F32),
            vmem((3, NA, 8, T), F32),
            vmem((NA, 8, T), F32),
            vmem((NA, N, 8, T), F32),
            vmem((2 * N, 4, NA * T), F32),
            vmem((8, NA * T), F32),
            vmem((HALF, 8, NA * T), F32),
            vmem((NA, 8, T), F32),
            vmem((NA + 1, N, 8, T), F32),
            vmem((N, 3, 8, T), F32),
            vmem((N, 4, T), F32),
            pltpu.SemaphoreType.DMA((10,)),
            pltpu.SemaphoreType.DMA((10,)),
        ],
        compiler_params=pltpu.CompilerParams(collective_id=0, has_side_effects=True),
        name="selected_inverse",
    )(
        ancestors,
        separator_inverse.reshape(3, T, 3 * T),
        panels.reshape(3, 8, 2 * HALF * T),
    )
    quad_rows = quad.reshape(2, HALF, 4, T).transpose(0, 2, 1, 3).reshape(2, 4, HALF * T)
    off_rows = off.transpose(0, 2, 1, 3).reshape(24, 2 * HALF * T)
    return off_rows, diag_inverse + quad_rows


def solution(mesh):
    return jax.shard_map(
        per_device,
        mesh=mesh,
        in_specs=(P("row", "col"), P(("row", "col"), None), P(None, ("row", "col"), None), P()),
        out_specs=(P(("row", "col"), None), P(None, ("row", "col"), None)),
        check_vma=False,
    )
```

time: 59.9 us -> 55.1 us (0.920)
  Pallas kernels: 55.6 us -> 51.3 us
    pallas_call x1, Pallas kernels: 55.6 us -> 51.3 us  [per_device(): pl.pallas_call(kernel, out_shape=(jax.ShapeDtypeStruct((3, N, 8, T), F32)...]
where the time goes in v3:
time: 55.1 us; the launch traced here: 54.9 us
  Pallas kernels  51.3 us (93%)
  local copies, waits for them, and re-layouts  1.62 us (3%)
  other arithmetic  1.38 us (3%)
  between operations  0.66 us (1%)
    pallas_call x1, Pallas kernels, per_device(): pl.pallas_call(kernel, out_shape=(jax.ShapeDtypeStruct((3, N, 8, T), F32)...  51.3 us
    unnamed x3, local copies, waits for them, and re-layouts  1.62 us
    add x1, other arithmetic, per_device(): return (off_rows, diag_inverse + quad_rows)  1.38 us

profile of v3, /device:TPU:1, one launch (start us, length us, event | category | flops | bytes accessed | tf_op | source)
XLA Modules:
  0.0 54.9 jit_solution(1218987448801022454)
XLA Ops:
  0.6 0.0 copy-start
  0.6 51.3 %selected_inverse.1 = (f32[3,16,8,128]{3,2,1,0:T(8,128)}, f32[16,4,128]{2,1,0:T(4,128)}) custom-call(s32[2,6]{1,0:T(2,128)} %anc.1, f32[3,128,384]{2,1,0:T(8,128)} %bitcast.10, f32[3,8,2048]{2,1,0:T(8,128)} %bitcast.12), custom_call_target="tpu_custom_call" | custom-call | tf_op jit(solution)/shard_map/selected_inverse/pallas_call | solution.py:303
  51.9 0.0 copy-done
  51.9 1.4 %add.3 = f32[2,4,1024]{2,1,0:T(4,128)} add(f32[2,4,1024]{2,1,0:T(4,128)S(1)} %copy-done, f32[2,4,1024]{2,1,0:T(4,128)} %bitcast.13) | non-fusion elementwise | flops 8192 | bytes 98304 | tf_op jit(solution)/shard_map/add | solution.py:343
  53.3 1.6 %copy.8 = f32[24,2048]{1,0:T(8,128)} copy(f32[24,2048]{1,0:T(8,128)} %bitcast.11) | data formatting | bytes 393216
Async XLA Ops:
  0.6 51.3 %copy-start = (f32[2,4,1024]{2,1,0:T(4,128)S(1)}, f32[2,4,1024]{2,1,0:T(4,128)}, u32[]{:S(2)}) copy-start(f32[2,4,1024]{2,1,0:T(4,128)} %param.6) | copy-start | bytes 98308

commit v4 on v3

--- a/solution.py
+++ b/solution.py
@@ -14,7 +14,7 @@
 NA = 6
 T = 128
 
-S1, S2, S3, P1, P2, X3, Y4, Q4, O5, D5 = range(10)
+S2, S3, P1, P2, X3, Y4, Q4, O4, O5, D5, S1 = range(11)
 
 
 def split(x):
@@ -53,6 +53,7 @@
     q_unit,
     q_buf,
     off_st,
+    off_cols,
     d_st,
     send,
     recv,
@@ -125,12 +126,14 @@
     loop(0, N - 1, greet)
     pl.semaphore_wait(barrier, 2 * (N - 1))
 
-    def send_s(i):
-        d = over_col(i)
-        remote(sep.at[:, pl.ds(8 * d, 8), :], s_rows.at[c], S1, (r, d)).start()
-
-    loop(0, N - 1, send_s)
-    local(sep.at[:, pl.ds(8 * c, 8), :], s_rows.at[c], S1).start()
+    for m in range(3):
+
+        def send_s(i, m=m):
+            d = over_col(i)
+            remote(sep.at[m, pl.ds(8 * d, 8), :], s_rows.at[m, c], S1 + m, (r, d)).start()
+
+        loop(0, N - 1, send_s)
+        local(sep.at[m, pl.ds(8 * c, 8), :], s_rows.at[m, c], S1 + m).start()
 
     def columns(d):
         return pan.at[:, :, pl.ds(pl.multiple_of(T * d, T), T)]
@@ -165,28 +168,29 @@
 
     loop(0, 3, send_p2)
 
-    take(recv.at[S1], s_rows)
-    for j in range(N):
-        for v in range(3):
-            s_by_tile[3 * j + v] = s_rows[j, :, :, T * v : T * v + T]
-    for t in range(2):
-        for l in range(NA):
-            s_col[t, l] = s_by_tile[anc[t, l]]
-
-    def send_s2(i):
-        d = over_row(i)
-        l = lax.rem(d, HALF)
-
-        @pl.when(l < NA)
+    for m in range(3):
+        take(recv.at[S1 + m], s_rows.at[m])
+        for j in range(N):
+            for v in range(3):
+                s_by_tile[m, 3 * j + v] = s_rows[m, j, :, T * v : T * v + T]
+        for t in range(2):
+            for l in range(NA):
+                s_col[m, t, l] = s_by_tile[m, anc[t, l]]
+
+        def send_s2(i, m=m):
+            d = over_row(i)
+            l = lax.rem(d, HALF)
+
+            @pl.when(l < NA)
+            def _():
+                src = s_col.at[m, lax.div(d, HALF), l]
+                remote(src, s_tiles.at[3 * r + m], S2, (d, c)).start()
+
+        loop(0, N - 1, send_s2)
+
+        @pl.when(b < NA)
         def _():
-            src = s_col.at[lax.div(d, HALF), l]
-            remote(src, s_tiles.at[pl.ds(3 * r, 3)], S2, (d, c)).start()
-
-    loop(0, N - 1, send_s2)
-
-    @pl.when(b < NA)
-    def _():
-        local(s_col.at[s, b], s_tiles.at[pl.ds(3 * r, 3)], S2).start()
+            local(s_col.at[m, s, b], s_tiles.at[3 * r + m], S2).start()
 
     take(recv.at[P2], p_perm)
     for k in range(NA):
@@ -229,34 +233,31 @@
     acc = jnp.zeros((NA * 8, T), F32)
     for l in range(NA):
         acc += dot3(split(s_fin[l].reshape(NA * 8, T)), split(x_buf[l].reshape(T, T)))
-    q_unit[...] = acc.reshape(NA, 8, T)
+    q_unit[0:NA] = acc.reshape(NA, 8, T)
+    q_unit[NA] = jnp.zeros((8, T), F32)
 
     def send_q(i):
         d = over_col(i)
-        remote(q_unit, q_buf.at[pl.ds(0, NA), c], Q4, (r, d)).start()
+        remote(q_unit.at[pl.ds(0, NA)], q_buf.at[:, c], Q4, (r, d)).start()
 
     loop(0, N - 1, send_q)
-    q_buf[0:NA, pl.ds(c, 1)] = q_unit[...][:, None]
-    q_buf[NA] = jnp.zeros((N, 8, T), F32)
+    q_buf[:, pl.ds(c, 1)] = q_unit[0:NA][:, None]
+
+    for t in range(NT):
+        off_st[t] = -q_unit[place[t]]
+
+    def send_off(i):
+        d = over_row(i)
+        remote(off_st.at[pl.ds(3 * d, 3)], off_cols.at[r], O4, (d, c)).start()
+
+    loop(0, N - 1, send_off)
+    local(off_st.at[pl.ds(3 * r, 3)], off_cols.at[r], O4).start()
 
     take(recv.at[Y4], y_buf)
     y_halves = split(y_buf[...].reshape(HALF * 8, NA * T))
-    take(recv.at[Q4], q_buf.at[pl.ds(0, NA), pl.ds(0, N - 1)])
-
-    for q in range(3):
-        piece = 3 * c + q
-        m, o = lax.div(piece, N), lax.rem(piece, N)
-        for j in range(N):
-            off_st[j, q] = -q_buf[place[3 * j + m], o]
-
-    def send_off(i):
-        d = over_row(i)
-        remote(off_st.at[d], off.at[:, r], O5, (d, c)).start()
-
-    loop(0, N - 1, send_off)
-    local(off_st.at[r], off.at[:, r], O5).start()
-
-    acc = dot3(y_halves, split(q_buf[0:NA].reshape(NA * T, T)))
+    take(recv.at[Q4], q_buf.at[:, pl.ds(0, N - 1)])
+
+    acc = dot3(y_halves, split(q_buf[...].reshape(NA * T, T)))
     d_st[...] = acc.reshape(N, 4, T)
 
     def send_d(i):
@@ -266,12 +267,21 @@
     loop(0, N - 1, send_d)
     local(d_st.at[r], quad.at[r], D5).start()
 
-    take(send.at[S1], s_rows.at[pl.ds(0, N - 1)])
+    take(recv.at[O4], off_cols)
+
+    def send_off2(m):
+        piece = N * m + c
+        push(off_cols.at[:, m], off.at[lax.rem(piece, 3)], O5, r, lax.div(piece, 3))
+
+    loop(0, 3, send_off2)
+
+    for m in range(3):
+        take(send.at[S1 + m], s_rows.at[m, pl.ds(0, N - 1)])
     take(send.at[P1], p_cols.at[pl.ds(0, N - 1)])
     take(send.at[X3], x_buf.at[:, pl.ds(0, N - 1)])
     take(send.at[Y4], y_buf.at[pl.ds(0, HALF - 1)])
     take(send.at[Q4], x_buf.at[:, pl.ds(0, N - 1)])
-    take(send.at[O5], off_st.at[pl.ds(0, N - 1)])
+    take(send.at[O4], off_cols.at[pl.ds(0, N - 1)])
     take(send.at[D5], d_st.at[pl.ds(0, N - 1)])
 
     @pl.when(b < NA)
@@ -288,13 +298,20 @@
     @pl.when(own)
     def _():
         take(send.at[P2], p_perm.at[pl.ds(0, 2)])
+        take(send.at[O5], off_st.at[pl.ds(0, 2 * N)])
 
     @pl.when(jnp.logical_not(own))
     def _():
         take(send.at[P2], p_perm)
+        take(send.at[O5], off_st)
 
     take(recv.at[O5], off)
     take(recv.at[D5], quad)
+
+
+def finish(off, quad, diag, off_out, diag_out):
+    off_out[...] = off[...]
+    diag_out[...] = diag[...] + quad[...]
 
 
 def per_device(separator_inverse, panels, diag_inverse, ancestors):
@@ -310,9 +327,9 @@
         out_specs=(hbm, pl.BlockSpec(memory_space=pltpu.VMEM)),
         scratch_shapes=[
             pltpu.SMEM((NT,), jnp.int32),
-            vmem((N, 3, 8, 3 * T), F32),
-            vmem((NT, 3, 8, T), F32),
-            vmem((2, NA, 3, 8, T), F32),
+            vmem((3, N, 8, 3 * T), F32),
+            vmem((3, NT, 8, T), F32),
+            vmem((3, 2, NA, 8, T), F32),
             vmem((NT, 8, T), F32),
             vmem((NA, 8, T), F32),
             vmem((NA, NA, 8, T), F32),
@@ -324,12 +341,13 @@
             vmem((2 * N, 4, NA * T), F32),
             vmem((8, NA * T), F32),
             vmem((HALF, 8, NA * T), F32),
-            vmem((NA, 8, T), F32),
-            vmem((NA + 1, N, 8, T), F32),
+            vmem((NA + 1, 8, T), F32),
+            vmem((NA, N, 8, T), F32),
+            vmem((NT, 8, T), F32),
             vmem((N, 3, 8, T), F32),
             vmem((N, 4, T), F32),
-            pltpu.SemaphoreType.DMA((10,)),
-            pltpu.SemaphoreType.DMA((10,)),
+            pltpu.SemaphoreType.DMA((13,)),
+            pltpu.SemaphoreType.DMA((13,)),
         ],
         compiler_params=pltpu.CompilerParams(collective_id=0, has_side_effects=True),
         name="selected_inverse",
@@ -338,9 +356,20 @@
         separator_inverse.reshape(3, T, 3 * T),
         panels.reshape(3, 8, 2 * HALF * T),
     )
-    quad_rows = quad.reshape(2, HALF, 4, T).transpose(0, 2, 1, 3).reshape(2, 4, HALF * T)
-    off_rows = off.transpose(0, 2, 1, 3).reshape(24, 2 * HALF * T)
-    return off_rows, diag_inverse + quad_rows
+    diag = diag_inverse.reshape(2, 4, HALF, T).transpose(0, 2, 1, 3).reshape(N, 4, T)
+    in_vmem = pl.BlockSpec(memory_space=pltpu.VMEM)
+    off, diag = pl.pallas_call(
+        finish,
+        out_shape=(
+            jax.ShapeDtypeStruct((3, N, 8, T), F32),
+            jax.ShapeDtypeStruct((N, 4, T), F32),
+        ),
+        in_specs=[in_vmem, in_vmem, in_vmem],
+        out_specs=(in_vmem, in_vmem),
+        name="finish",
+    )(off, quad, diag)
+    diag = diag.reshape(2, HALF, 4, T).transpose(0, 2, 1, 3).reshape(2, 4, HALF * T)
+    return off.transpose(0, 2, 1, 3).reshape(24, 2 * HALF * T), diag
 
 
 def solution(mesh):

time: 55.1 us -> 52.2 us (0.947)
  local copies, waits for them, and re-layouts: 1.62 us -> 0 us
  other arithmetic: 1.38 us -> 0 us
    pallas_call x0 -> x1, Pallas kernels: none -> 1.65 us  [per_device(): pl.pallas_call(finish, out_shape=(jax.ShapeDtypeStruct((3, N, 8, T), F32)...]
    unnamed x3 -> x0, local copies, waits for them, and re-layouts: 1.62 us -> none
    pallas_call x1, Pallas kernels: 51.3 us -> 49.8 us  [per_device(): pl.pallas_call(kernel, out_shape=(jax.ShapeDtypeStruct((3, N, 8, T), F32)...]
    add x1 -> x0, other arithmetic: 1.38 us -> none  [per_device(): return (off_rows, diag_inverse + quad_rows)]
where the time goes in v4:
time: 52.2 us; the launch traced here: 52 us
  Pallas kernels  51.4 us (98%)
  between operations  0.64 us (1%)
    pallas_call x1, Pallas kernels, per_device(): pl.pallas_call(kernel, out_shape=(jax.ShapeDtypeStruct((3, N, 8, T), F32)...  49.8 us
    pallas_call x1, Pallas kernels, per_device(): pl.pallas_call(finish, out_shape=(jax.ShapeDtypeStruct((3, N, 8, T), F32)...  1.65 us

profile of v4, /device:TPU:1, one launch (start us, length us, event | category | flops | bytes accessed | tf_op | source)
XLA Modules:
  0.0 52.0 jit_solution(11123493528425260990)
XLA Ops:
  0.6 49.8 %selected_inverse.1 = (f32[3,16,8,128]{3,2,1,0:T(8,128)}, f32[16,4,128]{2,1,0:T(4,128)}) custom-call(s32[2,6]{1,0:T(2,128)} %anc.1, f32[3,128,384]{2,1,0:T(8,128)} %bitcast.15, f32[3,8,2048]{2,1,0:T(8,128)} %bitcast.16), custom_call_target="tpu_custom_call" | custom-call | tf_op jit(solution)/shard_map/selected_inverse/pallas_call | solution.py:320
  50.4 1.6 %finish.1 = (f32[3,16,8,128]{3,2,1,0:T(8,128)}, f32[16,4,128]{2,1,0:T(4,128)}) custom-call(f32[3,16,8,128]{3,2,1,0:T(8,128)} %get-tuple-element.6.off, f32[16,4,128]{2,1,0:T(4,128)} %get-tuple-element.7.quad, f32[16,4,128]{2,1,0:T(4,128)} %bitcast.17), custom_call_target="tpu_custom_call" | custom-call | tf_op jit(solution)/shard_map/finish/pallas_call | solution.py:361

commit v5 on v4

--- a/solution.py
+++ b/solution.py
@@ -14,7 +14,7 @@
 NA = 6
 T = 128
 
-S2, S3, P1, P2, X3, Y4, Q4, O4, O5, D5, S1 = range(11)
+X4, Q5, S2, S3, P1, P2, X3, Y4, Q4, O4, O5, D5, S1 = range(13)
 
 
 def split(x):
@@ -30,9 +30,9 @@
 
 
 def kernel(
-    anc,
-    sep,
-    pan,
+    anc_hbm,
+    sep_hbm,
+    pan_hbm,
     off,
     quad,
     place,
@@ -55,6 +55,10 @@
     off_st,
     off_cols,
     d_st,
+    anc,
+    sep,
+    pan,
+    fetch,
     send,
     recv,
 ):
@@ -62,6 +66,9 @@
     c = lax.axis_index("col")
     s = lax.div(r, HALF)
     b = lax.rem(r, HALF)
+    chip = lax.div(c, 2)
+    core = lax.rem(c, 2)
+    sibling = c + 1 - 2 * core
 
     def remote(src, dst, i, device):
         return pltpu.make_async_remote_copy(
@@ -107,6 +114,12 @@
             + lax.rem(c + core, 2)
         )
 
+    def over_chips(i):
+        j = HALF - 1 - i
+        half, along = lax.div(j, 4), lax.rem(j, 4)
+        along = lax.div(along * (along + 1), 2)
+        return 8 * lax.rem(lax.div(c, 8) + half, 2) + 2 * lax.rem(chip + along, 4) + core
+
     def over_row(i):
         j = lax.div(i, 2)
         z = 4 + (1 - 2 * lax.rem(j, 2)) * lax.div(j + 1, 2)
@@ -124,6 +137,14 @@
             pl.semaphore_signal(barrier, inc=1, device_id=device, device_id_type=MESH)
 
     loop(0, N - 1, greet)
+    for m in range(3):
+        pltpu.make_async_copy(sep_hbm.at[m], sep.at[m], fetch.at[m]).start()
+    pltpu.make_async_copy(pan_hbm, pan, fetch.at[3]).start()
+    pltpu.make_async_copy(anc_hbm, anc, fetch.at[4]).start()
+    for m in range(3):
+        take(fetch.at[m], sep.at[m])
+    take(fetch.at[3], pan)
+    pltpu.make_async_copy(anc_hbm, anc, fetch.at[4]).wait()
     pl.semaphore_wait(barrier, 2 * (N - 1))
 
     for m in range(3):
@@ -197,11 +218,11 @@
         p_unit[k] = p_perm[anc[s, k] - 3 * row_of[k], k]
 
     def send_x(i):
-        d = over_col(i)
-        remote(p_unit, x_buf.at[:, c], X3, (r, d)).start()
-
-    loop(0, N - 1, send_x)
-    x_buf[:, pl.ds(c, 1)] = p_unit[...][:, None]
+        d = over_chips(i)
+        remote(p_unit, x_buf.at[:, chip, core], X3, (r, d)).start()
+
+    loop(0, HALF - 1, send_x)
+    x_buf[:, pl.ds(chip, 1), pl.ds(core, 1)] = p_unit[...][:, None, None]
 
     @pl.when(b < NA)
     def _():
@@ -216,7 +237,9 @@
         loop(0, HALF - 1, send_s3)
         local(s_unit, s_fin.at[b], S3).start()
 
-    take(recv.at[X3], x_buf.at[:, pl.ds(0, N - 1)])
+    take(recv.at[X3], x_buf.at[:, pl.ds(0, HALF - 1), 0])
+    remote(x_buf.at[:, :, core], x_buf.at[:, :, core], X4, (r, sibling)).start()
+    take(recv.at[X4], x_buf.at[:, :, 0])
     for k in range(NA):
         x_t[:, :, T * k : T * (k + 1)] = x_buf[k].reshape(T, T).T.reshape(2 * N, 4, T)
     y_unit[0:4] = x_t[c]
@@ -278,9 +301,10 @@
     for m in range(3):
         take(send.at[S1 + m], s_rows.at[m, pl.ds(0, N - 1)])
     take(send.at[P1], p_cols.at[pl.ds(0, N - 1)])
-    take(send.at[X3], x_buf.at[:, pl.ds(0, N - 1)])
+    take(send.at[X3], x_buf.at[:, pl.ds(0, HALF - 1), 0])
+    take(send.at[X4], x_buf.at[:, :, 0])
     take(send.at[Y4], y_buf.at[pl.ds(0, HALF - 1)])
-    take(send.at[Q4], x_buf.at[:, pl.ds(0, N - 1)])
+    take(send.at[Q4], q_buf.at[:, pl.ds(0, N - 1)])
     take(send.at[O4], off_cols.at[pl.ds(0, N - 1)])
     take(send.at[D5], d_st.at[pl.ds(0, N - 1)])
 
@@ -323,8 +347,8 @@
             jax.ShapeDtypeStruct((3, N, 8, T), F32),
             jax.ShapeDtypeStruct((N, 4, T), F32),
         ),
-        in_specs=[pl.BlockSpec(memory_space=pltpu.SMEM), hbm, hbm],
-        out_specs=(hbm, pl.BlockSpec(memory_space=pltpu.VMEM)),
+        in_specs=[hbm, hbm, hbm],
+        out_specs=(hbm, hbm),
         scratch_shapes=[
             pltpu.SMEM((NT,), jnp.int32),
             vmem((3, N, 8, 3 * T), F32),
@@ -337,7 +361,7 @@
             vmem((3, NA, 8, T), F32),
             vmem((3, NA, 8, T), F32),
             vmem((NA, 8, T), F32),
-            vmem((NA, N, 8, T), F32),
+            vmem((NA, HALF, 2, 8, T), F32),
             vmem((2 * N, 4, NA * T), F32),
             vmem((8, NA * T), F32),
             vmem((HALF, 8, NA * T), F32),
@@ -346,8 +370,12 @@
             vmem((NT, 8, T), F32),
             vmem((N, 3, 8, T), F32),
             vmem((N, 4, T), F32),
-            pltpu.SemaphoreType.DMA((13,)),
-            pltpu.SemaphoreType.DMA((13,)),
+            pltpu.SMEM((2, NA), jnp.int32),
+            vmem((3, T, 3 * T), F32),
+            vmem((3, 8, 2 * HALF * T), F32),
+            pltpu.SemaphoreType.DMA((5,)),
+            pltpu.SemaphoreType.DMA((15,)),
+            pltpu.SemaphoreType.DMA((15,)),
         ],
         compiler_params=pltpu.CompilerParams(collective_id=0, has_side_effects=True),
         name="selected_inverse",

time: 52.2 us -> 50.4 us (0.966)
  Pallas kernels: 51.4 us -> 49.6 us
    pallas_call x1, Pallas kernels: 49.8 us -> 48 us  [per_device(): pl.pallas_call(kernel, out_shape=(jax.ShapeDtypeStruct((3, N, 8, T), F32)...]
where the time goes in v5:
time: 50.4 us; the launch traced here: 50.3 us
  Pallas kernels  49.6 us (98%)
  between operations  0.64 us (1%)
    pallas_call x1, Pallas kernels, per_device(): pl.pallas_call(kernel, out_shape=(jax.ShapeDtypeStruct((3, N, 8, T), F32)...  48 us
    pallas_call x1, Pallas kernels, per_device(): pl.pallas_call(finish, out_shape=(jax.ShapeDtypeStruct((3, N, 8, T), F32)...  1.65 us

profile of v5, /device:TPU:1, one launch (start us, length us, event | category | flops | bytes accessed | tf_op | source)
XLA Modules:
  0.0 50.3 jit_solution(159406160000615519)
XLA Ops:
  0.6 48.0 %selected_inverse.1 = (f32[3,16,8,128]{3,2,1,0:T(8,128)}, f32[16,4,128]{2,1,0:T(4,128)}) custom-call(s32[2,6]{1,0:T(2,128)} %anc_hbm.1, f32[3,128,384]{2,1,0:T(8,128)} %bitcast.15, f32[3,8,2048]{2,1,0:T(8,128)} %bitcast.16), custom_call_target="tpu_custom_call" | custom-call | tf_op jit(solution)/shard_map/selected_inverse/pallas_call | solution.py:344
  48.6 1.6 %finish.1 = (f32[3,16,8,128]{3,2,1,0:T(8,128)}, f32[16,4,128]{2,1,0:T(4,128)}) custom-call(f32[3,16,8,128]{3,2,1,0:T(8,128)} %get-tuple-element.6.off, f32[16,4,128]{2,1,0:T(4,128)} %get-tuple-element.7.quad, f32[16,4,128]{2,1,0:T(4,128)} %bitcast.17), custom_call_target="tpu_custom_call" | custom-call | tf_op jit(solution)/shard_map/finish/pallas_call | solution.py:389

commit v6 on v5

--- a/solution.py
+++ b/solution.py
@@ -13,6 +13,7 @@
 NT = 48
 NA = 6
 T = 128
+CH = ((0, 1), (1, 3))
 
 X4, Q5, S2, S3, P1, P2, X3, Y4, Q4, O4, O5, D5, S1 = range(13)
 
@@ -133,7 +134,7 @@
     barrier = pltpu.get_barrier_semaphore()
 
     def greet(i):
-        for device in ((over_row(i), c), (r, over_col(i))):
+        for device in ((r, over_col(i)), (over_row(i), c)):
             pl.semaphore_signal(barrier, inc=1, device_id=device, device_id_type=MESH)
 
     loop(0, N - 1, greet)
@@ -147,14 +148,16 @@
     pltpu.make_async_copy(anc_hbm, anc, fetch.at[4]).wait()
     pl.semaphore_wait(barrier, 2 * (N - 1))
 
-    for m in range(3):
-
-        def send_s(i, m=m):
+    for lo, hi in CH:
+
+        def send_s(i, lo=lo, hi=hi):
             d = over_col(i)
-            remote(sep.at[m, pl.ds(8 * d, 8), :], s_rows.at[m, c], S1 + m, (r, d)).start()
+            src = sep.at[pl.ds(lo, hi - lo), pl.ds(8 * d, 8), :]
+            remote(src, s_rows.at[pl.ds(lo, hi - lo), c], S1 + lo, (r, d)).start()
 
         loop(0, N - 1, send_s)
-        local(sep.at[m, pl.ds(8 * c, 8), :], s_rows.at[m, c], S1 + m).start()
+        src = sep.at[pl.ds(lo, hi - lo), pl.ds(8 * c, 8), :]
+        local(src, s_rows.at[pl.ds(lo, hi - lo), c], S1 + lo).start()
 
     def columns(d):
         return pan.at[:, :, pl.ds(pl.multiple_of(T * d, T), T)]
@@ -189,29 +192,31 @@
 
     loop(0, 3, send_p2)
 
-    for m in range(3):
-        take(recv.at[S1 + m], s_rows.at[m])
-        for j in range(N):
-            for v in range(3):
-                s_by_tile[m, 3 * j + v] = s_rows[m, j, :, T * v : T * v + T]
-        for t in range(2):
-            for l in range(NA):
-                s_col[m, t, l] = s_by_tile[m, anc[t, l]]
-
-        def send_s2(i, m=m):
+    for lo, hi in CH:
+        take(recv.at[S1 + lo], s_rows.at[pl.ds(lo, hi - lo)])
+        for m in range(lo, hi):
+            for j in range(N):
+                for v in range(3):
+                    s_by_tile[m, 3 * j + v] = s_rows[m, j, :, T * v : T * v + T]
+            for t in range(2):
+                for l in range(NA):
+                    s_col[t, l, m] = s_by_tile[m, anc[t, l]]
+
+        def send_s2(i, lo=lo, hi=hi):
             d = over_row(i)
             l = lax.rem(d, HALF)
 
             @pl.when(l < NA)
             def _():
-                src = s_col.at[m, lax.div(d, HALF), l]
-                remote(src, s_tiles.at[3 * r + m], S2, (d, c)).start()
+                src = s_col.at[lax.div(d, HALF), l, pl.ds(lo, hi - lo)]
+                remote(src, s_tiles.at[pl.ds(3 * r + lo, hi - lo)], S2, (d, c)).start()
 
         loop(0, N - 1, send_s2)
 
         @pl.when(b < NA)
         def _():
-            local(s_col.at[m, s, b], s_tiles.at[3 * r + m], S2).start()
+            src = s_col.at[s, b, pl.ds(lo, hi - lo)]
+            local(src, s_tiles.at[pl.ds(3 * r + lo, hi - lo)], S2).start()
 
     take(recv.at[P2], p_perm)
     for k in range(NA):
@@ -260,11 +265,11 @@
     q_unit[NA] = jnp.zeros((8, T), F32)
 
     def send_q(i):
-        d = over_col(i)
-        remote(q_unit.at[pl.ds(0, NA)], q_buf.at[:, c], Q4, (r, d)).start()
-
-    loop(0, N - 1, send_q)
-    q_buf[:, pl.ds(c, 1)] = q_unit[0:NA][:, None]
+        d = over_chips(i)
+        remote(q_unit.at[pl.ds(0, NA)], q_buf.at[:, chip, core], Q4, (r, d)).start()
+
+    loop(0, HALF - 1, send_q)
+    q_buf[:, pl.ds(chip, 1), pl.ds(core, 1)] = q_unit[0:NA][:, None, None]
 
     for t in range(NT):
         off_st[t] = -q_unit[place[t]]
@@ -278,7 +283,9 @@
 
     take(recv.at[Y4], y_buf)
     y_halves = split(y_buf[...].reshape(HALF * 8, NA * T))
-    take(recv.at[Q4], q_buf.at[:, pl.ds(0, N - 1)])
+    take(recv.at[Q4], q_buf.at[:, pl.ds(0, HALF - 1), 0])
+    remote(q_buf.at[:, :, core], q_buf.at[:, :, core], Q5, (r, sibling)).start()
+    take(recv.at[Q5], q_buf.at[:, :, 0])
 
     acc = dot3(y_halves, split(q_buf[...].reshape(NA * T, T)))
     d_st[...] = acc.reshape(N, 4, T)
@@ -298,13 +305,14 @@
 
     loop(0, 3, send_off2)
 
-    for m in range(3):
-        take(send.at[S1 + m], s_rows.at[m, pl.ds(0, N - 1)])
+    for lo, hi in CH:
+        take(send.at[S1 + lo], s_rows.at[pl.ds(lo, hi - lo), pl.ds(0, N - 1)])
     take(send.at[P1], p_cols.at[pl.ds(0, N - 1)])
     take(send.at[X3], x_buf.at[:, pl.ds(0, HALF - 1), 0])
     take(send.at[X4], x_buf.at[:, :, 0])
     take(send.at[Y4], y_buf.at[pl.ds(0, HALF - 1)])
-    take(send.at[Q4], q_buf.at[:, pl.ds(0, N - 1)])
+    take(send.at[Q4], q_buf.at[:, pl.ds(0, HALF - 1), 0])
+    take(send.at[Q5], q_buf.at[:, :, 0])
     take(send.at[O4], off_cols.at[pl.ds(0, N - 1)])
     take(send.at[D5], d_st.at[pl.ds(0, N - 1)])
 
@@ -353,7 +361,7 @@
             pltpu.SMEM((NT,), jnp.int32),
             vmem((3, N, 8, 3 * T), F32),
             vmem((3, NT, 8, T), F32),
-            vmem((3, 2, NA, 8, T), F32),
+            vmem((2, NA, 3, 8, T), F32),
             vmem((NT, 8, T), F32),
             vmem((NA, 8, T), F32),
             vmem((NA, NA, 8, T), F32),
@@ -366,7 +374,7 @@
             vmem((8, NA * T), F32),
             vmem((HALF, 8, NA * T), F32),
             vmem((NA + 1, 8, T), F32),
-            vmem((NA, N, 8, T), F32),
+            vmem((NA, HALF, 2, 8, T), F32),
             vmem((NT, 8, T), F32),
             vmem((N, 3, 8, T), F32),
             vmem((N, 4, T), F32),

time: 50.4 us -> 49.6 us (0.984)
  Pallas kernels: 49.6 us -> 48.5 us
    pallas_call x1, Pallas kernels: 48 us -> 46.8 us  [per_device(): pl.pallas_call(kernel, out_shape=(jax.ShapeDtypeStruct((3, N, 8, T), F32)...]
where the time goes in v6:
time: 49.6 us; the launch traced here: 49.1 us
  Pallas kernels  48.5 us (98%)
  between operations  0.64 us (1%)
    pallas_call x1, Pallas kernels, per_device(): pl.pallas_call(kernel, out_shape=(jax.ShapeDtypeStruct((3, N, 8, T), F32)...  46.8 us
    pallas_call x1, Pallas kernels, per_device(): pl.pallas_call(finish, out_shape=(jax.ShapeDtypeStruct((3, N, 8, T), F32)...  1.65 us

profile of v6, /device:TPU:1, one launch (start us, length us, event | category | flops | bytes accessed | tf_op | source)
XLA Modules:
  0.0 49.1 jit_solution(9419811481421326293)
XLA Ops:
  0.6 46.8 %selected_inverse.1 = (f32[3,16,8,128]{3,2,1,0:T(8,128)}, f32[16,4,128]{2,1,0:T(4,128)}) custom-call(s32[2,6]{1,0:T(2,128)} %anc_hbm.1, f32[3,128,384]{2,1,0:T(8,128)} %bitcast.15, f32[3,8,2048]{2,1,0:T(8,128)} %bitcast.16), custom_call_target="tpu_custom_call" | custom-call | tf_op jit(solution)/shard_map/selected_inverse/pallas_call | solution.py:352
  47.5 1.6 %finish.1 = (f32[3,16,8,128]{3,2,1,0:T(8,128)}, f32[16,4,128]{2,1,0:T(4,128)}) custom-call(f32[3,16,8,128]{3,2,1,0:T(8,128)} %get-tuple-element.6.off, f32[16,4,128]{2,1,0:T(4,128)} %get-tuple-element.7.quad, f32[16,4,128]{2,1,0:T(4,128)} %bitcast.17), custom_call_target="tpu_custom_call" | custom-call | tf_op jit(solution)/shard_map/finish/pallas_call | solution.py:397

commit v7 on v6

--- a/solution.py
+++ b/solution.py
@@ -131,6 +131,9 @@
         z = lax.div(j * (j + 1), 2)
         return HALF * s + 2 * lax.rem(lax.div(b, 2) + z, 4) + lax.rem(b + 1 + i, 2)
 
+    def tile(buf, k):
+        return jnp.concatenate([buf[o % 2, o // 2, k] for o in range(N)])
+
     barrier = pltpu.get_barrier_semaphore()
 
     def greet(i):
@@ -224,10 +227,10 @@
 
     def send_x(i):
         d = over_chips(i)
-        remote(p_unit, x_buf.at[:, chip, core], X3, (r, d)).start()
+        remote(p_unit, x_buf.at[core, chip], X3, (r, d)).start()
 
     loop(0, HALF - 1, send_x)
-    x_buf[:, pl.ds(chip, 1), pl.ds(core, 1)] = p_unit[...][:, None, None]
+    x_buf[core, chip] = p_unit[...]
 
     @pl.when(b < NA)
     def _():
@@ -242,11 +245,11 @@
         loop(0, HALF - 1, send_s3)
         local(s_unit, s_fin.at[b], S3).start()
 
-    take(recv.at[X3], x_buf.at[:, pl.ds(0, HALF - 1), 0])
-    remote(x_buf.at[:, :, core], x_buf.at[:, :, core], X4, (r, sibling)).start()
-    take(recv.at[X4], x_buf.at[:, :, 0])
+    take(recv.at[X3], x_buf.at[0, pl.ds(0, HALF - 1)])
+    remote(x_buf.at[core], x_buf.at[core], X4, (r, sibling)).start()
+    take(recv.at[X4], x_buf.at[0])
     for k in range(NA):
-        x_t[:, :, T * k : T * (k + 1)] = x_buf[k].reshape(T, T).T.reshape(2 * N, 4, T)
+        x_t[:, :, T * k : T * (k + 1)] = tile(x_buf, k).T.reshape(2 * N, 4, T)
     y_unit[0:4] = x_t[c]
     y_unit[4:8] = x_t[N + c]
 
@@ -260,16 +263,16 @@
     take(recv.at[S3], s_fin)
     acc = jnp.zeros((NA * 8, T), F32)
     for l in range(NA):
-        acc += dot3(split(s_fin[l].reshape(NA * 8, T)), split(x_buf[l].reshape(T, T)))
+        acc += dot3(split(s_fin[l].reshape(NA * 8, T)), split(tile(x_buf, l)))
     q_unit[0:NA] = acc.reshape(NA, 8, T)
     q_unit[NA] = jnp.zeros((8, T), F32)
 
     def send_q(i):
         d = over_chips(i)
-        remote(q_unit.at[pl.ds(0, NA)], q_buf.at[:, chip, core], Q4, (r, d)).start()
+        remote(q_unit.at[pl.ds(0, NA)], q_buf.at[core, chip], Q4, (r, d)).start()
 
     loop(0, HALF - 1, send_q)
-    q_buf[:, pl.ds(chip, 1), pl.ds(core, 1)] = q_unit[0:NA][:, None, None]
+    q_buf[core, chip] = q_unit[0:NA]
 
     for t in range(NT):
         off_st[t] = -q_unit[place[t]]
@@ -281,13 +284,13 @@
     loop(0, N - 1, send_off)
     local(off_st.at[pl.ds(3 * r, 3)], off_cols.at[r], O4).start()
 
+    take(recv.at[Q4], q_buf.at[0, pl.ds(0, HALF - 1)])
+    remote(q_buf.at[core], q_buf.at[core], Q5, (r, sibling)).start()
     take(recv.at[Y4], y_buf)
     y_halves = split(y_buf[...].reshape(HALF * 8, NA * T))
-    take(recv.at[Q4], q_buf.at[:, pl.ds(0, HALF - 1), 0])
-    remote(q_buf.at[:, :, core], q_buf.at[:, :, core], Q5, (r, sibling)).start()
-    take(recv.at[Q5], q_buf.at[:, :, 0])
-
-    acc = dot3(y_halves, split(q_buf[...].reshape(NA * T, T)))
+    take(recv.at[Q5], q_buf.at[0])
+
+    acc = dot3(y_halves, split(jnp.concatenate([tile(q_buf, k) for k in range(NA)])))
     d_st[...] = acc.reshape(N, 4, T)
 
     def send_d(i):
@@ -308,11 +311,11 @@
     for lo, hi in CH:
         take(send.at[S1 + lo], s_rows.at[pl.ds(lo, hi - lo), pl.ds(0, N - 1)])
     take(send.at[P1], p_cols.at[pl.ds(0, N - 1)])
-    take(send.at[X3], x_buf.at[:, pl.ds(0, HALF - 1), 0])
-    take(send.at[X4], x_buf.at[:, :, 0])
+    take(send.at[X3], x_buf.at[0, pl.ds(0, HALF - 1)])
+    take(send.at[X4], x_buf.at[0])
     take(send.at[Y4], y_buf.at[pl.ds(0, HALF - 1)])
-    take(send.at[Q4], q_buf.at[:, pl.ds(0, HALF - 1), 0])
-    take(send.at[Q5], q_buf.at[:, :, 0])
+    take(send.at[Q4], q_buf.at[0, pl.ds(0, HALF - 1)])
+    take(send.at[Q5], q_buf.at[0])
     take(send.at[O4], off_cols.at[pl.ds(0, N - 1)])
     take(send.at[D5], d_st.at[pl.ds(0, N - 1)])
 
@@ -369,12 +372,12 @@
             vmem((3, NA, 8, T), F32),
             vmem((3, NA, 8, T), F32),
             vmem((NA, 8, T), F32),
-            vmem((NA, HALF, 2, 8, T), F32),
+            vmem((2, HALF, NA, 8, T), F32),
             vmem((2 * N, 4, NA * T), F32),
             vmem((8, NA * T), F32),
             vmem((HALF, 8, NA * T), F32),
             vmem((NA + 1, 8, T), F32),
-            vmem((NA, HALF, 2, 8, T), F32),
+            vmem((2, HALF, NA, 8, T), F32),
             vmem((NT, 8, T), F32),
             vmem((N, 3, 8, T), F32),
             vmem((N, 4, T), F32),

time: 49.6 us -> 49.5 us (level)
  no operation moved by 1% of the time
where the time goes in v7:
time: 49.5 us; the launch traced here: 49.1 us
  Pallas kernels  48.5 us (98%)
  between operations  0.64 us (1%)
    pallas_call x1, Pallas kernels, per_device(): pl.pallas_call(kernel, out_shape=(jax.ShapeDtypeStruct((3, N, 8, T), F32)...  46.8 us
    pallas_call x1, Pallas kernels, per_device(): pl.pallas_call(finish, out_shape=(jax.ShapeDtypeStruct((3, N, 8, T), F32)...  1.65 us

profile of v7, /device:TPU:1, one launch (start us, length us, event | category | flops | bytes accessed | tf_op | source)
XLA Modules:
  0.0 49.1 jit_solution(12883334453308946748)
XLA Ops:
  0.6 46.8 %selected_inverse.1 = (f32[3,16,8,128]{3,2,1,0:T(8,128)}, f32[16,4,128]{2,1,0:T(4,128)}) custom-call(s32[2,6]{1,0:T(2,128)} %anc_hbm.1, f32[3,128,384]{2,1,0:T(8,128)} %bitcast.15, f32[3,8,2048]{2,1,0:T(8,128)} %bitcast.16), custom_call_target="tpu_custom_call" | custom-call | tf_op jit(solution)/shard_map/selected_inverse/pallas_call | solution.py:355
  47.5 1.6 %finish.1 = (f32[3,16,8,128]{3,2,1,0:T(8,128)}, f32[16,4,128]{2,1,0:T(4,128)}) custom-call(f32[3,16,8,128]{3,2,1,0:T(8,128)} %get-tuple-element.6.off, f32[16,4,128]{2,1,0:T(4,128)} %get-tuple-element.7.quad, f32[16,4,128]{2,1,0:T(4,128)} %bitcast.17), custom_call_target="tpu_custom_call" | custom-call | tf_op jit(solution)/shard_map/finish/pallas_call | solution.py:400
